TPU v7x, 32 devices: a whole 2x2x4 slice. The times are simulated.
32 devices in a mesh: parts: 2 (over y), blk: 8 (over z, x), sub: 2 (over core).
Axes of the slice: x: 2, y: 2, z: 4, core: 2. Of those that a mesh axis runs over, the one named last changes fastest.
Arguments:
- embeddings: bfloat16 [24576, 1024], P(('parts', 'blk', 'sub')), parts along dimension 0, may hold values from -6 to 6
- labels: int32 [24576], P(('parts', 'blk', 'sub')), parts along dimension 0, may hold values from 0 to 127, as said below
Outputs:
- dedup_weight: float32 [24576], P(('parts', 'blk', 'sub')), parts along dimension 0
- cluster_mass: float32 [256], P('parts'), parts along dimension 0
There are 2 independent parts, one for each index of `parts`. A program takes and returns all parts, laid end to end along the dimension named above; each array names one. Nothing has to cross between parts.
Inputs may be any that keep to these rules, and one draw needn't show every extreme that they name: `labels`: every label of 0 to 127 occurs.
All inputs are finite; a program needn't handle non-finite values.
Results may differ from a plain program's by a relative error of at most 0.0003.
Values may be sent and summed in bfloat16 or wider, within the bound.
A program may use at most 64 MiB of HBM per device.

v0:
```python
import jax
import jax.numpy as jnp
from jax import lax
from jax.sharding import PartitionSpec as P

CLUSTERS = 128
ROUNDS = 3


TAU = 25.0


def swapped(value, axis, apart):
    mask = 2**apart
    pairs = [(source, source ^ mask) for source in range(lax.axis_size(axis))]
    return lax.ppermute(value, axis, pairs)


def kernel_tile(rows, row_lab, cols, col_lab):
    score = jnp.einsum("id,jd->ij", rows, cols, preferred_element_type=jnp.float32) / rows.shape[1]
    value = jnp.exp(TAU * (score - 1.0))
    return jnp.where(row_lab[:, None] == col_lab[None, :], value, 0.0)


def partner_piece(pair, mask):
    for bit in range(mask.bit_length()):
        if mask >> bit & 1:
            pair = swapped((pair[0], pair[1]), "blk", bit)
    return pair


def sums_back(column, mask):
    for bit in range(mask.bit_length()):
        if mask >> bit & 1:
            column = swapped(column, "blk", bit)
    return column


def per_device(embeddings, labels):
    count = embeddings.shape[0]
    block_emb, block_lab = (
        lax.all_gather(embeddings, "sub", axis=0, tiled=True),
        lax.all_gather(labels, "sub", axis=0, tiled=True),
    )
    density = jnp.sum(kernel_tile(embeddings, labels, block_emb, block_lab), axis=1)
    place = lax.axis_index("blk")
    half = lax.axis_index("sub")
    for mask in range(1, ROUNDS + 1):
        top_bit = mask.bit_length() - 1
        lower = place >> top_bit & 1 == 0
        start = jnp.where(lower, (1 - half) * count, half * count)
        send_emb = lax.dynamic_slice_in_dim(block_emb, start, count, 0)
        send_lab = lax.dynamic_slice_in_dim(block_lab, start, count, 0)
        other_emb, other_lab = partner_piece((send_emb, send_lab), mask)
        tile = kernel_tile(embeddings, labels, other_emb, other_lab)
        returned = sums_back(jnp.sum(tile, axis=0), mask)
        turned = swapped(returned, "sub", 0)
        density = density + jnp.sum(tile, axis=1) + jnp.where(lower, turned, returned)
    weight = 1.0 / density
    ident = jnp.arange(CLUSTERS, dtype=jnp.int32)
    local_mass = jnp.sum(jnp.where(labels[:, None] == ident[None, :], weight[:, None], 0.0), axis=0)
    cluster_mass = lax.psum(local_mass, ("blk", "sub"))
    return (weight, cluster_mass)


def solution(mesh):
    in_specs = (P(("parts", "blk", "sub"), None), P(("parts", "blk", "sub")))
    out_specs = (P(("parts", "blk", "sub")), P("parts"))
    return jax.shard_map(
        per_device, mesh=mesh, in_specs=in_specs, out_specs=out_specs, check_vma=False
    )
```

profile of v0, /device:TPU:0, one launch (start us, length us, event | category | flops | bytes accessed | tf_op | source)
XLA Modules:
  0.0 191.2 jit_solution(7212062031268630499)
XLA Ops:
  7.2 0.0 all-gather.3.cloned.1.call-start
  7.2 0.7 all-gather.3.cloned.1.call-update
  7.9 0.0 copy-start.3
  7.9 0.0 copy-start.1
  7.9 16.5 %all-gather.3.cloned.1.call-done = bf16[1536,1024]{1,0:T(8,128)(2,1)} async-done(((bf16[768,1024]{1,0:T(8,128)(2,1)}), bf16[1536,1024]{1,0:T(8,128)(2,1)}) %all-gather.3.cloned.1.call-update) | async-done | bytes 3145744 | tf_op jit(solution)/shard_map/all_gather | solution.py:42
  24.4 3.4 %constant_dynamic-slice_fusion.1 = (bf16[768,1024]{1,0:T(8,128)(2,1)}, bf16[768,1024]{1,0:T(8,128)(2,1)S(1)}) fusion(bf16[1536,1024]{1,0:T(8,128)(2,1)} %all-gather.3.cloned.1.call-done, s32[]{:T(128)S(6)} %select_n.56, s32[]{:T(128)S(6)} %select_n.61), kind=kLoop, calls=%fused_computation.8 | loop fusion | bytes 6291464 | tf_op jit(solution)/shard_map/dynamic_slice | solution.py:52
  27.8 1.7 collective-permute-start.10
  29.5 0.3 collective-permute-start.1
  29.8 35.3 %collective-permute-done.10 = bf16[768,1024]{1,0:T(8,128)(2,1)} collective-permute-done((bf16[768,1024]{1,0:T(8,128)(2,1)S(1)}, bf16[768,1024]{1,0:T(8,128)(2,1)}, u32[]{:S(2)}, u32[]{:S(2)}) %collective-permute-start.10) | collective-permute-done | bytes 1572896 | tf_op jit(solution)/shard_map/ppermute | solution.py:16
  65.1 1.7 collective-permute-start.11
  66.8 0.3 collective-permute-start.5
  67.1 0.0 copy-done.3
  67.1 1.8 all-gather
  69.0 0.1 fusion.3
  69.1 1.7 collective-permute-start
  70.8 0.3 collective-permute-start.8
  71.1 27.2 %collective-permute-done = s32[768]{0:T(1024)S(1)} collective-permute-done((s32[768]{0:T(1024)S(1)}, s32[768]{0:T(1024)S(1)}, u32[]{:S(2)}, u32[]{:S(2)}) %collective-permute-start) | collective-permute-done | bytes 3104 | tf_op jit(solution)/shard_map/ppermute | solution.py:16
  98.2 1.8 collective-permute-start.4
  100.0 0.0 collective-permute-done.8
  100.0 0.3 collective-permute-start.9
  100.3 0.0 collective-permute-done.1
  100.3 0.0 copy-done.1
  100.3 3.2 %fusion = (f32[768]{0:T(1024)S(1)}, f32[768]{0:T(1024)S(1)}) fusion(bf16[768,1024]{1,0:T(8,128)(2,1)} %collective-permute-done.1, bf16[768,1024]{1,0:T(8,128)(2,1)S(1)} %copy-done.1, s32[768]{0:T(1024)S(1)} %collective-permute-done, s32[768]{0:T(1024)S(1)} %copy-done.3), kind=kOutput, calls=%fused_computation.9 | convolution fusion | flops 1212086784 | bytes 3158016 | tf_op jit(solution)/shard_map/id,jd->ij/dot_general | solution.py:20
  103.5 1.8 collective-permute-start.2
  105.3 29.1 %collective-permute-done.9 = s32[768]{0:T(1024)S(1)} collective-permute-done((s32[768]{0:T(1024)S(1)}, s32[768]{0:T(1024)S(1)}, u32[]{:S(2)}, u32[]{:S(2)}) %collective-permute-start.9) | collective-permute-done | bytes 3104 | tf_op jit(solution)/shard_map/ppermute | solution.py:16
  134.4 0.0 collective-permute-done.11
  134.4 3.2 %fusion.2 = (f32[768]{0:T(1024)S(1)}, f32[768]{0:T(1024)S(1)}) fusion(bf16[768,1024]{1,0:T(8,128)(2,1)} %collective-permute-done.11, bf16[768,1024]{1,0:T(8,128)(2,1)S(1)} %copy-done.1, s32[768]{0:T(1024)S(1)} %collective-permute-done.9, s32[768]{0:T(1024)S(1)} %copy-done.3), kind=kOutput, calls=%fused_computation.11 | convolution fusion | flops 1212086784 | bytes 3158016 | tf_op jit(solution)/shard_map/id,jd->ij/dot_general | solution.py:20
  137.6 1.8 collective-permute-start.12
  139.3 0.0 collective-permute-done.4
  139.3 0.0 collective-permute-done.5
  139.3 3.2 %fusion.1 = (f32[768]{0:T(1024)S(1)}, f32[768]{0:T(1024)S(1)}) fusion(bf16[768,1024]{1,0:T(8,128)(2,1)} %collective-permute-done.5, bf16[768,1024]{1,0:T(8,128)(2,1)S(1)} %copy-done.1, s32[768]{0:T(1024)S(1)} %collective-permute-done.4, s32[768]{0:T(1024)S(1)} %copy-done.3), kind=kOutput, calls=%fused_computation.10 | convolution fusion | flops 1212086784 | bytes 3158016 | tf_op jit(solution)/shard_map/id,jd->ij/dot_general | solution.py:20
  142.5 1.6 collective-permute-start.6
  144.1 0.0 collective-permute-done.12
  144.1 0.5 collective-permute-start.13
  144.6 0.0 collective-permute-done.2
  144.6 0.0 collective-permute-start.3
  144.6 1.6 collective-permute-done.6
  146.2 0.0 collective-permute-start.7
  146.2 1.5 collective-permute-done.13
  147.7 0.0 collective-permute-start.14
  147.7 3.5 %select_reduce_fusion = f32[768]{0:T(1024)S(1)} fusion(bf16[768,1024]{1,0:T(8,128)(2,1)S(1)} %copy-done.1, bf16[1536,1024]{1,0:T(8,128)(2,1)S(1)} %copy-done, s32[1536]{0:T(1024)S(1)} %reshape.11, s32[768]{0:T(1024)S(1)} %copy-done.3), kind=kOutput, calls=%fused_computation | convolution fusion | flops 2422996224 | bytes 4730880 | tf_op jit(solution)/shard_map/id,jd->ij/dot_general | solution.py:20
  151.2 0.0 collective-permute-done.3
  151.2 0.0 collective-permute-done.7
  151.2 0.0 collective-permute-done.14
  151.3 0.0 copy-start.2
  151.3 0.3 select_reduce_fusion.1
  151.6 32.8 %psum.7 = f32[128]{0:T(128)} all-reduce(f32[128]{0:T(128)S(1)} %select_reduce_fusion.1), channel_id=1, replica_groups=mesh['parts'=2,'blk'=8,'sub'=2] {'blk','sub'}, use_global_device_ids=true, to_apply=%region_8.9 | all-reduce | flops 128 | bytes 1024 | tf_op jit(solution)/shard_map/psum | solution.py:62
  184.3 0.0 copy-done.2
  (6 shorter events, 0.1 us)
Async XLA Ops:
  7.2 17.2 %all-gather.3.cloned.1.call-start = ((), (), s32[]{:S(2)}) async-start(), calls=%async_computation | async-start | bytes 4718592 | tf_op jit(solution)/shard_map/all_gather | solution.py:42
  7.9 59.2 %copy-start.3 = (s32[768]{0:T(1024)S(1)}, s32[768]{0:T(1024)}, u32[]{:S(2)}) copy-start(s32[768]{0:T(1024)} %param.3) | copy-start | bytes 9220
  7.9 92.4 %copy-start.1 = (bf16[768,1024]{1,0:T(8,128)(2,1)S(1)}, bf16[768,1024]{1,0:T(8,128)(2,1)}, u32[]{:S(2)}) copy-start(bf16[768,1024]{1,0:T(8,128)(2,1)} %param.2) | copy-start | bytes 4718596
  27.8 37.3 %collective-permute-start.10 = (bf16[768,1024]{1,0:T(8,128)(2,1)S(1)}, bf16[768,1024]{1,0:T(8,128)(2,1)}, u32[]{:S(2)}, u32[]{:S(2)}) collective-permute-start(bf16[768,1024]{1,0:T(8,128)(2,1)S(1)} %get-tuple-element.9), channel_id=1, source_target_pairs={{0,2},{2,0},{4,6},{6,4},{8,10},{10,8},{12,14},{14,12},{1,3},{3,1},... | collective-permute-start | bytes 4718600 | tf_op jit(solution)/shard_map/ppermute | solution.py:16
  29.5 70.8 %collective-permute-start.1 = (bf16[768,1024]{1,0:T(8,128)(2,1)}, bf16[768,1024]{1,0:T(8,128)(2,1)}, u32[]{:S(2)}, u32[]{:S(2)}) collective-permute-start(bf16[768,1024]{1,0:T(8,128)(2,1)} %get-tuple-element.8), channel_id=1, source_target_pairs={{0,2},{2,0},{4,6},{6,4},{8,10},{10,8},{12,14},{14,12},{1,3},{3,1},... | collective-permute-start | bytes 4718600 | tf_op jit(solution)/shard_map/ppermute | solution.py:16
  65.1 69.3 %collective-permute-start.11 = (bf16[768,1024]{1,0:T(8,128)(2,1)}, bf16[768,1024]{1,0:T(8,128)(2,1)}, u32[]{:S(2)}, u32[]{:S(2)}) collective-permute-start(bf16[768,1024]{1,0:T(8,128)(2,1)} %collective-permute-done.10), channel_id=1, source_target_pairs={{0,4},{2,6},{4,0},{6,2},{8,12},{10,14},{12,8},{14,10},{1,5},{3,7},... | collective-permute-start | bytes 4718600 | tf_op jit(solution)/shard_map/ppermute | solution.py:16
  66.8 72.5 %collective-permute-start.5 = (bf16[768,1024]{1,0:T(8,128)(2,1)S(1)}, bf16[768,1024]{1,0:T(8,128)(2,1)}, u32[]{:S(2)}, u32[]{:S(2)}) collective-permute-start(bf16[768,1024]{1,0:T(8,128)(2,1)S(1)} %get-tuple-element.9), channel_id=1, source_target_pairs={{0,4},{2,6},{4,0},{6,2},{8,12},{10,14},{12,8},{14,10},{1,5},{3,7},... | collective-permute-start | bytes 4718600 | tf_op jit(solution)/shard_map/ppermute | solution.py:16
  69.1 29.2 %collective-permute-start = (s32[768]{0:T(1024)S(1)}, s32[768]{0:T(1024)S(1)}, u32[]{:S(2)}, u32[]{:S(2)}) collective-permute-start(s32[768]{0:T(1024)S(1)} %get-tuple-element.10), channel_id=1, source_target_pairs={{0,2},{2,0},{4,6},{6,4},{8,10},{10,8},{12,14},{14,12},{1,3},{3,1},... | collective-permute-start | bytes 9224 | tf_op jit(solution)/shard_map/ppermute | solution.py:16
  70.8 29.2 %collective-permute-start.8 = (s32[768]{0:T(1024)S(1)}, s32[768]{0:T(1024)S(1)}, u32[]{:S(2)}, u32[]{:S(2)}) collective-permute-start(s32[768]{0:T(1024)S(1)} %get-tuple-element.11), channel_id=1, source_target_pairs={{0,2},{2,0},{4,6},{6,4},{8,10},{10,8},{12,14},{14,12},{1,3},{3,1},... | collective-permute-start | bytes 9224 | tf_op jit(solution)/shard_map/ppermute | solution.py:16
  98.2 41.1 %collective-permute-start.4 = (s32[768]{0:T(1024)S(1)}, s32[768]{0:T(1024)S(1)}, u32[]{:S(2)}, u32[]{:S(2)}) collective-permute-start(s32[768]{0:T(1024)S(1)} %get-tuple-element.11), channel_id=1, source_target_pairs={{0,4},{2,6},{4,0},{6,2},{8,12},{10,14},{12,8},{14,10},{1,5},{3,7},... | collective-permute-start | bytes 9224 | tf_op jit(solution)/shard_map/ppermute | solution.py:16
  100.0 34.4 %collective-permute-start.9 = (s32[768]{0:T(1024)S(1)}, s32[768]{0:T(1024)S(1)}, u32[]{:S(2)}, u32[]{:S(2)}) collective-permute-start(s32[768]{0:T(1024)S(1)} %collective-permute-done.8), channel_id=1, source_target_pairs={{0,4},{2,6},{4,0},{6,2},{8,12},{10,14},{12,8},{14,10},{1,5},{3,7},... | collective-permute-start | bytes 9224 | tf_op jit(solution)/shard_map/ppermute | solution.py:16
  103.5 41.2 %collective-permute-start.2 = (f32[768]{0:T(1024)S(1)}, f32[768]{0:T(1024)S(1)}, u32[]{:S(2)}, u32[]{:S(2)}) collective-permute-start(f32[768]{0:T(1024)S(1)} %get-tuple-element.3), channel_id=1, source_target_pairs={{0,2},{2,0},{4,6},{6,4},{8,10},{10,8},{12,14},{14,12},{1,3},{3,1},... | collective-permute-start | bytes 9224 | tf_op jit(solution)/shard_map/ppermute | solution.py:16
  137.5 10.2 %copy-start = (bf16[1536,1024]{1,0:T(8,128)(2,1)S(1)}, bf16[1536,1024]{1,0:T(8,128)(2,1)}, u32[]{:S(2)}) copy-start(bf16[1536,1024]{1,0:T(8,128)(2,1)} %all-gather.3.cloned.1.call-done) | copy-start | bytes 9437188
  137.6 6.6 %collective-permute-start.12 = (f32[768]{0:T(1024)S(1)}, f32[768]{0:T(1024)S(1)}, u32[]{:S(2)}, u32[]{:S(2)}) collective-permute-start(f32[768]{0:T(1024)S(1)} %get-tuple-element.7), channel_id=1, source_target_pairs={{0,2},{2,0},{4,6},{6,4},{8,10},{10,8},{12,14},{14,12},{1,3},{3,1},... | collective-permute-start | bytes 9224 | tf_op jit(solution)/shard_map/ppermute | solution.py:16
  142.5 3.7 %collective-permute-start.6 = (f32[768]{0:T(1024)S(1)}, f32[768]{0:T(1024)S(1)}, u32[]{:S(2)}, u32[]{:S(2)}) collective-permute-start(f32[768]{0:T(1024)S(1)} %get-tuple-element.5), channel_id=1, source_target_pairs={{0,4},{2,6},{4,0},{6,2},{8,12},{10,14},{12,8},{14,10},{1,5},{3,7},... | collective-permute-start | bytes 9224 | tf_op jit(solution)/shard_map/ppermute | solution.py:16
  144.1 3.6 %collective-permute-start.13 = (f32[768]{0:T(1024)S(1)}, f32[768]{0:T(1024)S(1)}, u32[]{:S(2)}, u32[]{:S(2)}) collective-permute-start(f32[768]{0:T(1024)S(1)} %collective-permute-done.12), channel_id=1, source_target_pairs={{0,4},{2,6},{4,0},{6,2},{8,12},{10,14},{12,8},{14,10},{1,5},{3,7},... | collective-permute-start | bytes 9224 | tf_op jit(solution)/shard_map/ppermute | solution.py:16
  144.6 6.6 %collective-permute-start.3 = (f32[768]{0:T(1024)S(1)}, f32[768]{0:T(1024)S(1)}, u32[]{:S(2)}, u32[]{:S(2)}) collective-permute-start(f32[768]{0:T(1024)S(1)} %collective-permute-done.2), channel_id=1, source_target_pairs={{0,1},{1,0},{2,3},{3,2},{4,5},{5,4},{6,7},{7,6},{8,9},{9,8},{10,11... | collective-permute-start | bytes 9224 | tf_op jit(solution)/shard_map/ppermute | solution.py:16
  146.2 5.0 %collective-permute-start.7 = (f32[768]{0:T(1024)S(1)}, f32[768]{0:T(1024)S(1)}, u32[]{:S(2)}, u32[]{:S(2)}) collective-permute-start(f32[768]{0:T(1024)S(1)} %collective-permute-done.6), channel_id=1, source_target_pairs={{0,1},{1,0},{2,3},{3,2},{4,5},{5,4},{6,7},{7,6},{8,9},{9,8},{10,11... | collective-permute-start | bytes 9224 | tf_op jit(solution)/shard_map/ppermute | solution.py:16
  147.7 3.5 %collective-permute-start.14 = (f32[768]{0:T(1024)S(1)}, f32[768]{0:T(1024)S(1)}, u32[]{:S(2)}, u32[]{:S(2)}) collective-permute-start(f32[768]{0:T(1024)S(1)} %collective-permute-done.13), channel_id=1, source_target_pairs={{0,1},{1,0},{2,3},{3,2},{4,5},{5,4},{6,7},{7,6},{8,9},{9,8},{10,11... | collective-permute-start | bytes 9224 | tf_op jit(solution)/shard_map/ppermute | solution.py:16
  151.3 33.0 %copy-start.2 = (f32[768]{0:T(1024)}, f32[768]{0:T(1024)S(1)}, u32[]{:S(2)}) copy-start(f32[768]{0:T(1024)S(1)} %add_divide_fusion) | copy-start | bytes 9220
Sparse Core Ops, SparseCore 0:
  9.5 14.8 all-gather.2
where the time goes:
time: 191 us
  waiting for transfers between devices  112 us (59%)
  blocking collectives  34.5 us (18%)
  between operations  14.1 us (7%)
  starting transfers between devices  13.8 us (7%)
  matrix products  13 us (7%)
  local copies, waits for them, and re-layouts  3.5 us (2%)
    ppermute x15, waiting for transfers between devices, swapped(): return lax.ppermute(value, axis, pairs)  94.7 us
    psum x1, blocking collectives, per_device(): cluster_mass = lax.psum(local_mass, ('blk', 'sub'))  32.8 us
    all_gather x1, waiting for transfers between devices, per_device(): lax.all_gather(embeddings, 'sub', axis=0, tiled=True)  16.5 us
    ppermute x15, starting transfers between devices, swapped(): return lax.ppermute(value, axis, pairs)  13.8 us
    dot_general x4, matrix products, kernel_tile(): jnp.einsum('id,jd->ij', rows, cols, preferred_element_type=jnp.float32)  13 us
  transfers between devices with their start and end apart: 16, of which 6 were waited for; matrix products, arithmetic and copies ran while one was open for 7% of the time, Pallas kernels for 0%

commit v1 on v0

v1 whole, which is shorter than its diff:
```python
import functools
import math

import jax
import jax.numpy as jnp
from jax import lax
from jax.experimental import pallas as pl
from jax.experimental.pallas import tpu as pltpu
from jax.sharding import PartitionSpec as P

CLUSTERS = 128
GROUP = 4
TAU = 25.0
MESH = pl.DeviceIdType.MESH
CHUNK = 256


def ring_swap(v):
    return v + lax.div(v, 2) - 2 * lax.div(v, 3)


def kernel(emb, lab, out_w, out_m, other, near, far, cross, labs, cols,
           near_sum, far_sum, cross_sum, send_buf, back,
           near_send, near_recv, far_send, far_recv, other_sem, cross_send,
           cross_recv, lab_send, lab_recv, back_send, back_recv):
    count, width = emb.shape
    n = count // CHUNK
    scale = TAU * math.log2(math.e) / width
    part = lax.axis_index("parts")
    blk = lax.axis_index("blk")
    core = lax.axis_index("sub")
    low = lax.rem(blk, GROUP)
    base = blk - low
    place = ring_swap(low)
    step = 1 - 2 * core

    def device(offset, c):
        return (part, base + ring_swap(lax.rem(place + offset + 2 * GROUP, GROUP)), c)

    me = place * 2 + core
    nxt = device(step, core)
    prv = device(-step, core)
    sib = device(0, 1 - core)
    opp = device(2, core)
    skew = device(step, 1 - core)

    def who(offset, c):
        return lax.rem(place + offset + 2 * GROUP, GROUP) * 2 + c

    barrier = pltpu.get_barrier_semaphore()
    others = [(o, x) for o in range(GROUP) for x in range(2) if (o, x) != (0, 0)]
    for o, x in others:
        pl.semaphore_signal(barrier, inc=1, device_id=device(o, x + core - 2 * x * core),
                            device_id_type=MESH)
    pl.semaphore_wait(barrier, len(others))

    def rows(c):
        return pl.ds(pl.multiple_of(c * CHUNK, CHUNK), CHUNK)

    def copy(src, dst, s, r, dev):
        return pltpu.make_async_remote_copy(src_ref=src, dst_ref=dst, send_sem=s, recv_sem=r,
                                            device_id=dev, device_id_type=MESH)

    def near_copy(c):
        return copy(emb.at[rows(c)], near.at[rows(c)], near_send.at[c], near_recv.at[c], nxt)

    def far_copy(c):
        return copy(near.at[rows(c)], far.at[rows(c)], far_send.at[c], far_recv.at[c], nxt)

    def cross_copy(c):
        return copy(near.at[rows(c)], cross.at[rows(c)], cross_send.at[c], cross_recv.at[c], sib)

    def other_copy():
        return copy(emb, other, other_sem.at[0], other_sem.at[1], sib)

    def lab_copy(k):
        o, x = others[k]
        c = x + core - 2 * x * core
        sent = copy(lab, labs.at[me], lab_send.at[k], lab_recv.at[me], device(o, c))
        src = who(o, c)
        got = copy(lab, labs.at[src], lab_send.at[k], lab_recv.at[src], device(o, c))
        return sent, got

    for k in range(len(others)):
        lab_copy(k)[0].start()

    @pl.loop(0, n)
    def _(c):
        near_copy(c).start()

    other_copy().start()

    def column(row):
        return jnp.broadcast_to(row, (128, count)).T

    own_lab = lab[...]
    cols[0] = column(own_lab)

    def tile(x, xlab, y, ylab):
        s = lax.dot_general(x, y, (((1,), (1,)), ((), ())), preferred_element_type=jnp.float32)
        v = jnp.exp2((s - float(width)) * scale)
        same = jnp.concatenate([xlab] * (count // 128), axis=1) == ylab
        return jnp.where(same, v, 0.0)

    def colsum(v):
        return jnp.sum(v, axis=0, keepdims=True)

    def rowpart(v):
        t = v[:, :128]
        for k in range(1, count // 128):
            t = t + v[:, k * 128:(k + 1) * 128]
        return t

    def own_tile(ref, slot, c):
        return tile(ref[rows(c), :], cols[slot, rows(c), :], emb[...], own_lab)

    zero = jnp.zeros((1, count), jnp.float32)
    own = lax.fori_loop(0, n, lambda c, a: a + colsum(own_tile(emb, 0, c)), zero)

    for k in range(len(others)):
        sent, got = lab_copy(k)
        got.wait_recv()
    cols[1] = column(labs[who(0, 1 - core)])
    cols[2] = column(labs[who(-step, core)])
    cols[3] = column(labs[who(step, 1 - core)])
    cols[4] = column(labs[who(2, core)])
    cross_lab = labs[who(step, 1 - core)]

    other_copy().wait_recv()
    own = lax.fori_loop(0, n, lambda c, a: a + colsum(own_tile(other, 1, c)), own)

    def near_step(c, a):
        near_copy(c).wait_recv()
        far_copy(c).start()
        cross_copy(c).start()
        v = own_tile(near, 2, c)
        near_sum[rows(c), :] = rowpart(v)
        return a + colsum(v)

    own = lax.fori_loop(0, n, near_step, own)

    def cross_step(c, a):
        cross_copy(c).wait_recv()
        return a + colsum(own_tile(cross, 3, c))

    own = lax.fori_loop(0, n, cross_step, own)
    cross_sum[...] = zero

    @pl.when(core == 1)
    def _():
        @pl.loop(0, n)
        def _(c):
            v = tile(near[rows(c), :], cols[2, rows(c), :], cross[...], cross_lab)
            near_sum[rows(c), :] += rowpart(v)
            cross_sum[...] += colsum(v)

    def back_copy(k, dev):
        return copy(send_buf.at[k], back.at[k], back_send.at[k], back_recv.at[k], dev)

    send_buf[0] = colsum(near_sum[...].T)
    back_copy(0, prv).start()

    def far_step(c, a):
        far_copy(c).wait_recv()

        @pl.when(core == 0)
        def _():
            v = tile(far[rows(c), :], cols[4, rows(c), :], cross[...], cross_lab)
            far_sum[rows(c), :] = rowpart(v)
            cross_sum[...] += colsum(v)

            @pl.when(c == n - 1)
            def _():
                send_buf[1] = colsum(far_sum[...].T)
                send_buf[2] = cross_sum[...]
                back_copy(1, opp).start()
                back_copy(2, skew).start()

        @pl.when((core == 1) & (c == 0))
        def _():
            send_buf[1] = zero
            send_buf[2] = cross_sum[...]
            back_copy(1, opp).start()
            back_copy(2, skew).start()

        return a + colsum(own_tile(far, 4, c))

    own = lax.fori_loop(0, n, far_step, own)

    for k, dev in enumerate((prv, opp, skew)):
        back_copy(k, dev).wait_recv()
        own = own + back[k]

    weight = 1.0 / own
    out_w[...] = weight
    ident = lax.broadcasted_iota(jnp.int32, (CLUSTERS, count), 0)
    out_m[...] = colsum(rowpart(jnp.where(ident == own_lab, weight, 0.0)).T)

    @pl.loop(0, n)
    def _(c):
        near_copy(c).wait_send()
        far_copy(c).wait_send()
        cross_copy(c).wait_send()

    other_copy().wait_send()
    for k in range(len(others)):
        lab_copy(k)[0].wait_send()
    for k, dev in enumerate((prv, opp, skew)):
        back_copy(k, dev).wait_send()


def per_device(embeddings, labels):
    count, width = embeddings.shape
    n = count // CHUNK
    f32, i32, bf16 = jnp.float32, jnp.int32, jnp.bfloat16
    dma = pltpu.SemaphoreType.DMA
    vmem = pl.BlockSpec(memory_space=pltpu.VMEM)
    weight, mass = pl.pallas_call(
        kernel,
        out_shape=(jax.ShapeDtypeStruct((1, count), f32), jax.ShapeDtypeStruct((1, CLUSTERS), f32)),
        in_specs=[vmem, vmem],
        out_specs=(vmem, vmem),
        scratch_shapes=[
            pltpu.VMEM((count, width), bf16),
            pltpu.VMEM((count, width), bf16),
            pltpu.VMEM((count, width), bf16),
            pltpu.VMEM((count, width), bf16),
            pltpu.VMEM((2 * GROUP, 1, count), i32),
            pltpu.VMEM((5, count, 128), i32),
            pltpu.VMEM((count, 128), f32),
            pltpu.VMEM((count, 128), f32),
            pltpu.VMEM((1, count), f32),
            pltpu.VMEM((3, 1, count), f32),
            pltpu.VMEM((3, 1, count), f32),
            dma((n,)), dma((n,)), dma((n,)), dma((n,)), dma((2,)), dma((n,)), dma((n,)),
            dma((2 * GROUP - 1,)), dma((2 * GROUP,)), dma((3,)), dma((3,)),
        ],
        compiler_params=pltpu.CompilerParams(
            collective_id=0, has_side_effects=True, vmem_limit_bytes=48 * 1024 * 1024),
        cost_estimate=pl.CostEstimate(flops=12 * count * count * width, bytes_accessed=2 * count * width,
                                      transcendentals=6 * count * count),
    )(embeddings, labels.reshape(1, count))
    return weight.reshape(count), lax.psum(mass.reshape(CLUSTERS), ("blk", "sub"))


def solution(mesh):
    in_specs = (P(("parts", "blk", "sub"), None), P(("parts", "blk", "sub")))
    out_specs = (P(("parts", "blk", "sub")), P("parts"))
    return jax.shard_map(
        per_device, mesh=mesh, in_specs=in_specs, out_specs=out_specs, check_vma=False
    )
```

time: 191 us -> 81.1 us (0.42)
  waiting for transfers between devices: 112 us -> 0 us
  Pallas kernels: 0 us -> 44.4 us
  starting transfers between devices: 13.8 us -> 0 us
  between operations: 14.1 us -> 0.64 us
  matrix products: 13 us -> 0 us
    ppermute x15 -> x0, waiting for transfers between devices: 94.7 us -> none  [swapped(): return lax.ppermute(value, axis, pairs)]
    pallas_call x0 -> x1, Pallas kernels: none -> 44.4 us  [per_device(): pl.pallas_call(kernel, out_shape=(jax.ShapeDtypeStruct((1, count), f32),...]
    all_gather x1 -> x0, waiting for transfers between devices: 16.5 us -> none  [per_device(): lax.all_gather(embeddings, 'sub', axis=0, tiled=True)]
    ppermute x15 -> x0, starting transfers between devices: 13.8 us -> none  [swapped(): return lax.ppermute(value, axis, pairs)]
    dot_general x4 -> x0, matrix products: 13 us -> none  [kernel_tile(): jnp.einsum('id,jd->ij', rows, cols, preferred_element_type=jnp.float32)]
    dynamic_slice x2 -> x0, local copies, waits for them, and re-layouts: 3.47 us -> none  [the longest x1 3.38 us: per_device(): send_emb = lax.dynamic_slice_in_dim(block_emb, start, count, 0)]
  transfers between devices with their start and end apart: 16 -> 0, of which waited for: 6 -> 0; matrix products, arithmetic and copies ran while one was open for 7% -> 0% of each run, Pallas kernels for 0% -> 0%
where the time goes in v1:
time: 81.1 us; the launch traced here: 80.9 us
  Pallas kernels  44.4 us (55%)
  blocking collectives  33.2 us (41%)
  local copies, waits for them, and re-layouts  2.1 us (3%)
    pallas_call x1, Pallas kernels, per_device(): pl.pallas_call(kernel, out_shape=(jax.ShapeDtypeStruct((1, count), f32),...  44.4 us
    psum x1, blocking collectives, per_device(): lax.psum(mass.reshape(CLUSTERS), ('blk', 'sub'))  33.2 us

profile of v1, /device:TPU:0, one launch (start us, length us, event | category | flops | bytes accessed | tf_op | source)
XLA Modules:
  0.0 80.9 jit_solution(3168282371213349488)
XLA Ops:
  0.6 0.7 reshape.13.lab
  1.3 0.0 copy-start
  1.3 1.4 %copy-done = bf16[768,1024]{1,0:T(8,128)(2,1)S(1)} copy-done((bf16[768,1024]{1,0:T(8,128)(2,1)S(1)}, bf16[768,1024]{1,0:T(8,128)(2,1)}, u32[]{:S(2)}) %copy-start) | copy-done | bytes 1572888
  2.7 44.4 %shard_map.41 = (f32[1,768]{1,0:T(1,128)S(1)}, f32[1,128]{1,0:T(1,128)S(1)}) custom-call(bf16[768,1024]{1,0:T(8,128)(2,1)S(1)} %copy-done, s32[1,768]{1,0:T(1,128)S(1)} %reshape.13.lab), custom_call_target="tpu_custom_call" | custom-call | flops 7247757312 | bytes 1572864 | tf_op jit(solution)/shard_map/pallas_call | solution.py:218
  47.1 33.2 %psum.7 = f32[128]{0:T(128)} all-reduce(f32[128]{0:T(128)S(1)} %bitcast.1), channel_id=1, replica_groups=mesh['parts'=2,'blk'=8,'sub'=2] {'blk','sub'}, use_global_device_ids=true, to_apply=%region_0.0 | all-reduce | flops 128 | bytes 1024 | tf_op jit(solution)/shard_map/psum | solution.py:243
  80.3 0.6 reduce
Async XLA Ops:
  1.3 1.4 %copy-start = (bf16[768,1024]{1,0:T(8,128)(2,1)S(1)}, bf16[768,1024]{1,0:T(8,128)(2,1)}, u32[]{:S(2)}) copy-start(bf16[768,1024]{1,0:T(8,128)(2,1)} %emb.1) | copy-start | bytes 4718596

commit v2 on v1

--- a/solution.py
+++ b/solution.py
@@ -19,10 +19,11 @@
     return v + lax.div(v, 2) - 2 * lax.div(v, 3)
 
 
-def kernel(emb, lab, out_w, out_m, other, near, far, cross, labs, cols,
+def kernel(src, lab1, out_w, out_m, emb, lab, masses, other, near, far, cross, labs, cols,
            near_sum, far_sum, cross_sum, send_buf, back,
            near_send, near_recv, far_send, far_recv, other_sem, cross_send,
-           cross_recv, lab_send, lab_recv, back_send, back_recv):
+           cross_recv, lab_send, lab_recv, back_send, back_recv,
+           local_sem, mass_send, mass_recv):
     count, width = emb.shape
     n = count // CHUNK
     scale = TAU * math.log2(math.e) / width
@@ -33,6 +34,11 @@
     base = blk - low
     place = ring_swap(low)
     step = 1 - 2 * core
+    total = 2 * lax.axis_size("blk")
+    index = 2 * blk + core
+    load = pltpu.make_async_copy(src, emb, local_sem.at[0])
+    load.start()
+    lab[...] = lab1[...].reshape(1, count)
 
     def device(offset, c):
         return (part, base + ring_swap(lax.rem(place + offset + 2 * GROUP, GROUP)), c)
@@ -47,12 +53,19 @@
     def who(offset, c):
         return lax.rem(place + offset + 2 * GROUP, GROUP) * 2 + c
 
+    others = [(o, x) for o in range(GROUP) for x in range(2) if (o, x) != (0, 0)]
+
+    def member(k):
+        t = lax.rem(index + k, total)
+        return t, (part, lax.div(t, 2), lax.rem(t, 2))
+
     barrier = pltpu.get_barrier_semaphore()
-    others = [(o, x) for o in range(GROUP) for x in range(2) if (o, x) != (0, 0)]
-    for o, x in others:
-        pl.semaphore_signal(barrier, inc=1, device_id=device(o, x + core - 2 * x * core),
-                            device_id_type=MESH)
-    pl.semaphore_wait(barrier, len(others))
+
+    @pl.loop(1, total)
+    def _(k):
+        pl.semaphore_signal(barrier, inc=1, device_id=member(k)[1], device_id_type=MESH)
+
+    pl.semaphore_wait(barrier, total - 1)
 
     def rows(c):
         return pl.ds(pl.multiple_of(c * CHUNK, CHUNK), CHUNK)
@@ -62,7 +75,7 @@
                                             device_id=dev, device_id_type=MESH)
 
     def near_copy(c):
-        return copy(emb.at[rows(c)], near.at[rows(c)], near_send.at[c], near_recv.at[c], nxt)
+        return copy(src.at[rows(c)], near.at[rows(c)], near_send.at[c], near_recv.at[c], nxt)
 
     def far_copy(c):
         return copy(near.at[rows(c)], far.at[rows(c)], far_send.at[c], far_recv.at[c], nxt)
@@ -71,7 +84,7 @@
         return copy(near.at[rows(c)], cross.at[rows(c)], cross_send.at[c], cross_recv.at[c], sib)
 
     def other_copy():
-        return copy(emb, other, other_sem.at[0], other_sem.at[1], sib)
+        return copy(src, other, other_sem.at[0], other_sem.at[1], sib)
 
     def lab_copy(k):
         o, x = others[k]
@@ -81,13 +94,12 @@
         got = copy(lab, labs.at[src], lab_send.at[k], lab_recv.at[src], device(o, c))
         return sent, got
 
-    for k in range(len(others)):
-        lab_copy(k)[0].start()
-
     @pl.loop(0, n)
     def _(c):
         near_copy(c).start()
 
+    for k in range(len(others)):
+        lab_copy(k)[0].start()
     other_copy().start()
 
     def column(row):
@@ -95,6 +107,7 @@
 
     own_lab = lab[...]
     cols[0] = column(own_lab)
+    load.wait()
 
     def tile(x, xlab, y, ylab):
         s = lax.dot_general(x, y, (((1,), (1,)), ((), ())), preferred_element_type=jnp.float32)
@@ -192,9 +205,20 @@
         own = own + back[k]
 
     weight = 1.0 / own
-    out_w[...] = weight
     ident = lax.broadcasted_iota(jnp.int32, (CLUSTERS, count), 0)
-    out_m[...] = colsum(rowpart(jnp.where(ident == own_lab, weight, 0.0)).T)
+    masses[index] = colsum(rowpart(jnp.where(ident == own_lab, weight, 0.0)).T)
+
+    def mass_copy(k):
+        t, dev = member(k)
+        sent = copy(masses.at[index], masses.at[index], mass_send.at[k], mass_recv.at[index], dev)
+        got = copy(masses.at[t], masses.at[t], mass_send.at[k], mass_recv.at[t], dev)
+        return sent, got
+
+    @pl.loop(1, total)
+    def _(k):
+        mass_copy(k)[0].start()
+
+    out_w[...] = weight.reshape(count)
 
     @pl.loop(0, n)
     def _(c):
@@ -208,19 +232,33 @@
     for k, dev in enumerate((prv, opp, skew)):
         back_copy(k, dev).wait_send()
 
+    @pl.loop(1, total)
+    def _(k):
+        mass_copy(k)[1].wait_recv()
+
+    out_m[...] = jnp.sum(masses[...], axis=0).reshape(CLUSTERS)
+
+    @pl.loop(1, total)
+    def _(k):
+        mass_copy(k)[0].wait_send()
+
 
 def per_device(embeddings, labels):
     count, width = embeddings.shape
     n = count // CHUNK
+    total = 2 * lax.axis_size("blk")
     f32, i32, bf16 = jnp.float32, jnp.int32, jnp.bfloat16
     dma = pltpu.SemaphoreType.DMA
     vmem = pl.BlockSpec(memory_space=pltpu.VMEM)
     weight, mass = pl.pallas_call(
         kernel,
-        out_shape=(jax.ShapeDtypeStruct((1, count), f32), jax.ShapeDtypeStruct((1, CLUSTERS), f32)),
-        in_specs=[vmem, vmem],
+        out_shape=(jax.ShapeDtypeStruct((count,), f32), jax.ShapeDtypeStruct((CLUSTERS,), f32)),
+        in_specs=[pl.BlockSpec(memory_space=pltpu.HBM), vmem],
         out_specs=(vmem, vmem),
         scratch_shapes=[
+            pltpu.VMEM((count, width), bf16),
+            pltpu.VMEM((1, count), i32),
+            pltpu.VMEM((total, 1, CLUSTERS), f32),
             pltpu.VMEM((count, width), bf16),
             pltpu.VMEM((count, width), bf16),
             pltpu.VMEM((count, width), bf16),
@@ -234,13 +272,14 @@
             pltpu.VMEM((3, 1, count), f32),
             dma((n,)), dma((n,)), dma((n,)), dma((n,)), dma((2,)), dma((n,)), dma((n,)),
             dma((2 * GROUP - 1,)), dma((2 * GROUP,)), dma((3,)), dma((3,)),
+            dma((1,)), dma((total,)), dma((total,)),
         ],
         compiler_params=pltpu.CompilerParams(
             collective_id=0, has_side_effects=True, vmem_limit_bytes=48 * 1024 * 1024),
         cost_estimate=pl.CostEstimate(flops=12 * count * count * width, bytes_accessed=2 * count * width,
                                       transcendentals=6 * count * count),
-    )(embeddings, labels.reshape(1, count))
-    return weight.reshape(count), lax.psum(mass.reshape(CLUSTERS), ("blk", "sub"))
+    )(embeddings, labels)
+    return weight, mass
 
 
 def solution(mesh):

time: 81.1 us -> 59.6 us (0.73)
  blocking collectives: 33.2 us -> 0 us
  Pallas kernels: 44.4 us -> 55.6 us
  local copies, waits for them, and re-layouts: 2.1 us -> 3.19 us
    psum x1 -> x0, blocking collectives: 33.2 us -> none  [per_device(): lax.psum(mass.reshape(CLUSTERS), ('blk', 'sub'))]
    pallas_call x1, Pallas kernels: 44.4 us -> 55.6 us  [per_device(): pl.pallas_call(kernel, out_shape=(jax.ShapeDtypeStruct((count,), f32), ja...]
    unnamed x2 -> x6, local copies, waits for them, and re-layouts: 1.41 us -> 3.19 us
where the time goes in v2:
time: 59.6 us; the launch traced here: 59.4 us
  Pallas kernels  55.6 us (93%)
  local copies, waits for them, and re-layouts  3.19 us (5%)
  between operations  0.65 us (1%)
    pallas_call x1, Pallas kernels, per_device(): pl.pallas_call(kernel, out_shape=(jax.ShapeDtypeStruct((count,), f32), ja...  55.6 us
    unnamed x6, local copies, waits for them, and re-layouts  3.19 us

profile of v2, /device:TPU:0, one launch (start us, length us, event | category | flops | bytes accessed | tf_op | source)
XLA Modules:
  0.0 59.4 jit_solution(8772862640810374052)
XLA Ops:
  0.6 0.0 copy-start
  0.6 1.4 %copy-done = bf16[768,1024]{1,0:T(8,128)(2,1)S(1)} copy-done((bf16[768,1024]{1,0:T(8,128)(2,1)S(1)}, bf16[768,1024]{1,0:T(8,128)(2,1)}, u32[]{:S(2)}) %copy-start) | copy-done | bytes 1572888
  2.0 0.0 copy-start.1
  2.0 0.7 %copy-done.1 = s32[768]{0:T(1024)S(1)} copy-done((s32[768]{0:T(1024)S(1)}, s32[768]{0:T(1024)}, u32[]{:S(2)}) %copy-start.1) | copy-done | bytes 3096
  2.7 55.6 %shard_map.41 = (f32[768]{0:T(1024)S(1)}, f32[128]{0:T(128)S(1)}) custom-call(bf16[768,1024]{1,0:T(8,128)(2,1)S(1)} %copy-done, s32[768]{0:T(1024)S(1)} %copy-done.1), custom_call_target="tpu_custom_call" | custom-call | flops 7247757312 | bytes 1572864 | tf_op jit(solution)/shard_map/pallas_call | solution.py:253
  58.3 0.6 %copy.6 = f32[768]{0:T(1024)} copy(f32[768]{0:T(1024)S(1)} %get-tuple-element.4) | data formatting | bytes 6144
  58.9 0.5 copy.7
Async XLA Ops:
  0.6 1.4 %copy-start = (bf16[768,1024]{1,0:T(8,128)(2,1)S(1)}, bf16[768,1024]{1,0:T(8,128)(2,1)}, u32[]{:S(2)}) copy-start(bf16[768,1024]{1,0:T(8,128)(2,1)} %src.1) | copy-start | bytes 4718596
  2.0 0.7 %copy-start.1 = (s32[768]{0:T(1024)S(1)}, s32[768]{0:T(1024)}, u32[]{:S(2)}) copy-start(s32[768]{0:T(1024)} %lab1.1) | copy-start | bytes 9220

commit v3 on v2

--- a/solution.py
+++ b/solution.py
@@ -94,12 +94,13 @@
         got = copy(lab, labs.at[src], lab_send.at[k], lab_recv.at[src], device(o, c))
         return sent, got
 
+    for k in range(len(others)):
+        lab_copy(k)[0].start()
+
     @pl.loop(0, n)
     def _(c):
         near_copy(c).start()
 
-    for k in range(len(others)):
-        lab_copy(k)[0].start()
     other_copy().start()
 
     def column(row):
@@ -139,9 +140,6 @@
     cols[4] = column(labs[who(2, core)])
     cross_lab = labs[who(step, 1 - core)]
 
-    other_copy().wait_recv()
-    own = lax.fori_loop(0, n, lambda c, a: a + colsum(own_tile(other, 1, c)), own)
-
     def near_step(c, a):
         near_copy(c).wait_recv()
         far_copy(c).start()
@@ -151,6 +149,9 @@
         return a + colsum(v)
 
     own = lax.fori_loop(0, n, near_step, own)
+
+    other_copy().wait_recv()
+    own = lax.fori_loop(0, n, lambda c, a: a + colsum(own_tile(other, 1, c)), own)
 
     def cross_step(c, a):
         cross_copy(c).wait_recv()
@@ -275,7 +276,7 @@
             dma((1,)), dma((total,)), dma((total,)),
         ],
         compiler_params=pltpu.CompilerParams(
-            collective_id=0, has_side_effects=True, vmem_limit_bytes=48 * 1024 * 1024),
+            collective_id=0, has_side_effects=True, vmem_limit_bytes=63 * 1024 * 1024),
         cost_estimate=pl.CostEstimate(flops=12 * count * count * width, bytes_accessed=2 * count * width,
                                       transcendentals=6 * count * count),
     )(embeddings, labels)

time: 59.6 us -> 54.6 us (0.916)
  Pallas kernels: 55.6 us -> 51.4 us
  local copies, waits for them, and re-layouts: 3.19 us -> 2.4 us
    pallas_call x1, Pallas kernels: 55.6 us -> 51.4 us  [per_device(): pl.pallas_call(kernel, out_shape=(jax.ShapeDtypeStruct((count,), f32), ja...]
    unnamed x6 -> x2, local copies, waits for them, and re-layouts: 3.19 us -> 2.4 us
where the time goes in v3:
time: 54.6 us; the launch traced here: 54.4 us
  Pallas kernels  51.4 us (94%)
  local copies, waits for them, and re-layouts  2.4 us (4%)
  between operations  0.64 us (1%)
    pallas_call x1, Pallas kernels, per_device(): pl.pallas_call(kernel, out_shape=(jax.ShapeDtypeStruct((count,), f32), ja...  51.4 us
    unnamed x2, local copies, waits for them, and re-layouts  2.4 us

profile of v3, /device:TPU:0, one launch (start us, length us, event | category | flops | bytes accessed | tf_op | source)
XLA Modules:
  0.0 54.4 jit_solution(4764036041093263752)
XLA Ops:
  0.6 51.4 %shard_map.41 = (f32[768]{0:T(1024)}, f32[128]{0:T(128)}) custom-call(bf16[768,1024]{1,0:T(8,128)(2,1)} %src.1, s32[768]{0:T(1024)} %lab1.1), custom_call_target="tpu_custom_call" | custom-call | flops 7247757312 | bytes 1572864 | tf_op jit(solution)/shard_map/pallas_call | solution.py:254
  52.0 1.3 %copy.6 = f32[768]{0:T(1024)} copy(f32[768]{0:T(1024)} %get-tuple-element.4) | data formatting | bytes 6144
  53.3 1.1 %copy.7 = f32[128]{0:T(128)} copy(f32[128]{0:T(128)} %get-tuple-element.5) | data formatting | bytes 1024

commit v4 on v3

--- a/solution.py
+++ b/solution.py
@@ -19,8 +19,8 @@
     return v + lax.div(v, 2) - 2 * lax.div(v, 3)
 
 
-def kernel(src, lab1, out_w, out_m, emb, lab, masses, other, near, far, cross, labs, cols,
-           near_sum, far_sum, cross_sum, send_buf, back,
+def kernel(src, lab1, out_w, out_m, emb, flat, lab, masses, other, near, far, cross, labs, cols,
+           near_sum, cross_sum, send_buf, back,
            near_send, near_recv, far_send, far_recv, other_sem, cross_send,
            cross_recv, lab_send, lab_recv, back_send, back_recv,
            local_sem, mass_send, mass_recv):
@@ -38,7 +38,8 @@
     index = 2 * blk + core
     load = pltpu.make_async_copy(src, emb, local_sem.at[0])
     load.start()
-    lab[...] = lab1[...].reshape(1, count)
+    load_lab = pltpu.make_async_copy(lab1, flat, local_sem.at[1])
+    load_lab.start()
 
     def device(offset, c):
         return (part, base + ring_swap(lax.rem(place + offset + 2 * GROUP, GROUP)), c)
@@ -65,6 +66,8 @@
     def _(k):
         pl.semaphore_signal(barrier, inc=1, device_id=member(k)[1], device_id_type=MESH)
 
+    load_lab.wait()
+    lab[...] = flat[...].reshape(1, count)
     pl.semaphore_wait(barrier, total - 1)
 
     def rows(c):
@@ -180,12 +183,11 @@
         @pl.when(core == 0)
         def _():
             v = tile(far[rows(c), :], cols[4, rows(c), :], cross[...], cross_lab)
-            far_sum[rows(c), :] = rowpart(v)
+            send_buf[1, :, rows(c)] = colsum(rowpart(v).T)
             cross_sum[...] += colsum(v)
 
             @pl.when(c == n - 1)
             def _():
-                send_buf[1] = colsum(far_sum[...].T)
                 send_buf[2] = cross_sum[...]
                 back_copy(1, opp).start()
                 back_copy(2, skew).start()
@@ -254,10 +256,11 @@
     weight, mass = pl.pallas_call(
         kernel,
         out_shape=(jax.ShapeDtypeStruct((count,), f32), jax.ShapeDtypeStruct((CLUSTERS,), f32)),
-        in_specs=[pl.BlockSpec(memory_space=pltpu.HBM), vmem],
+        in_specs=[pl.BlockSpec(memory_space=pltpu.HBM)] * 2,
         out_specs=(vmem, vmem),
         scratch_shapes=[
             pltpu.VMEM((count, width), bf16),
+            pltpu.VMEM((count,), i32),
             pltpu.VMEM((1, count), i32),
             pltpu.VMEM((total, 1, CLUSTERS), f32),
             pltpu.VMEM((count, width), bf16),
@@ -266,14 +269,13 @@
             pltpu.VMEM((count, width), bf16),
             pltpu.VMEM((2 * GROUP, 1, count), i32),
             pltpu.VMEM((5, count, 128), i32),
-            pltpu.VMEM((count, 128), f32),
             pltpu.VMEM((count, 128), f32),
             pltpu.VMEM((1, count), f32),
             pltpu.VMEM((3, 1, count), f32),
             pltpu.VMEM((3, 1, count), f32),
             dma((n,)), dma((n,)), dma((n,)), dma((n,)), dma((2,)), dma((n,)), dma((n,)),
             dma((2 * GROUP - 1,)), dma((2 * GROUP,)), dma((3,)), dma((3,)),
-            dma((1,)), dma((total,)), dma((total,)),
+            dma((2,)), dma((total,)), dma((total,)),
         ],
         compiler_params=pltpu.CompilerParams(
             collective_id=0, has_side_effects=True, vmem_limit_bytes=63 * 1024 * 1024),

time: 54.6 us -> 54 us (0.989)
  Pallas kernels: 51.4 us -> 50.7 us
    pallas_call x1, Pallas kernels: 51.4 us -> 50.7 us  [per_device(): pl.pallas_call(kernel, out_shape=(jax.ShapeDtypeStruct((count,), f32), ja...]
where the time goes in v4:
time: 54 us; the launch traced here: 53.7 us
  Pallas kernels  50.7 us (94%)
  local copies, waits for them, and re-layouts  2.4 us (4%)
  between operations  0.64 us (1%)
    pallas_call x1, Pallas kernels, per_device(): pl.pallas_call(kernel, out_shape=(jax.ShapeDtypeStruct((count,), f32), ja...  50.7 us
    unnamed x2, local copies, waits for them, and re-layouts  2.4 us

profile of v4, /device:TPU:0, one launch (start us, length us, event | category | flops | bytes accessed | tf_op | source)
XLA Modules:
  0.0 53.7 jit_solution(3371746044072031360)
XLA Ops:
  0.6 50.7 %shard_map.41 = (f32[768]{0:T(1024)}, f32[128]{0:T(128)}) custom-call(bf16[768,1024]{1,0:T(8,128)(2,1)} %src.1, s32[768]{0:T(1024)} %lab1.1), custom_call_target="tpu_custom_call" | custom-call | flops 7247757312 | bytes 1572864 | tf_op jit(solution)/shard_map/pallas_call | solution.py:256
  51.3 1.3 %copy.6 = f32[768]{0:T(1024)} copy(f32[768]{0:T(1024)} %get-tuple-element.4) | data formatting | bytes 6144
  52.6 1.1 %copy.7 = f32[128]{0:T(128)} copy(f32[128]{0:T(128)} %get-tuple-element.5) | data formatting | bytes 1024

commit v5 on v4

--- a/solution.py
+++ b/solution.py
@@ -36,8 +36,6 @@
     step = 1 - 2 * core
     total = 2 * lax.axis_size("blk")
     index = 2 * blk + core
-    load = pltpu.make_async_copy(src, emb, local_sem.at[0])
-    load.start()
     load_lab = pltpu.make_async_copy(lab1, flat, local_sem.at[1])
     load_lab.start()
 
@@ -62,10 +60,12 @@
 
     barrier = pltpu.get_barrier_semaphore()
 
-    @pl.loop(1, total)
+    @pl.loop(1, total, unroll=5 if (total - 1) % 5 == 0 else 1)
     def _(k):
         pl.semaphore_signal(barrier, inc=1, device_id=member(k)[1], device_id_type=MESH)
 
+    load = pltpu.make_async_copy(src, emb, local_sem.at[0])
+    load.start()
     load_lab.wait()
     lab[...] = flat[...].reshape(1, count)
     pl.semaphore_wait(barrier, total - 1)
@@ -217,7 +217,7 @@
         got = copy(masses.at[t], masses.at[t], mass_send.at[k], mass_recv.at[t], dev)
         return sent, got
 
-    @pl.loop(1, total)
+    @pl.loop(1, total, unroll=5 if (total - 1) % 5 == 0 else 1)
     def _(k):
         mass_copy(k)[0].start()
 
@@ -235,13 +235,13 @@
     for k, dev in enumerate((prv, opp, skew)):
         back_copy(k, dev).wait_send()
 
-    @pl.loop(1, total)
+    @pl.loop(1, total, unroll=5 if (total - 1) % 5 == 0 else 1)
     def _(k):
         mass_copy(k)[1].wait_recv()
 
     out_m[...] = jnp.sum(masses[...], axis=0).reshape(CLUSTERS)
 
-    @pl.loop(1, total)
+    @pl.loop(1, total, unroll=5 if (total - 1) % 5 == 0 else 1)
     def _(k):
         mass_copy(k)[0].wait_send()
 

time: 54 us -> 53.8 us (level)
  no operation moved by 1% of the time
where the time goes in v5:
time: 53.8 us; the launch traced here: 53.6 us
  Pallas kernels  50.5 us (94%)
  local copies, waits for them, and re-layouts  2.4 us (4%)
  between operations  0.64 us (1%)
    pallas_call x1, Pallas kernels, per_device(): pl.pallas_call(kernel, out_shape=(jax.ShapeDtypeStruct((count,), f32), ja...  50.5 us
    unnamed x2, local copies, waits for them, and re-layouts  2.4 us

profile of v5, /device:TPU:0, one launch (start us, length us, event | category | flops | bytes accessed | tf_op | source)
XLA Modules:
  0.0 53.6 jit_solution(7005887233226287542)
XLA Ops:
  0.6 50.5 %shard_map.41 = (f32[768]{0:T(1024)}, f32[128]{0:T(128)}) custom-call(bf16[768,1024]{1,0:T(8,128)(2,1)} %src.1, s32[768]{0:T(1024)} %lab1.1), custom_call_target="tpu_custom_call" | custom-call | flops 7247757312 | bytes 1572864 | tf_op jit(solution)/shard_map/pallas_call | solution.py:256
  51.2 1.3 %copy.6 = f32[768]{0:T(1024)} copy(f32[768]{0:T(1024)} %get-tuple-element.4) | data formatting | bytes 6144
  52.4 1.1 %copy.7 = f32[128]{0:T(128)} copy(f32[128]{0:T(128)} %get-tuple-element.5) | data formatting | bytes 1024
